TPU v7x, 32 devices: a whole 2x2x4 slice. The times are simulated.
32 devices in a mesh: elem: 4 (over z), tm: 8 (over y, x, core).
Axes of the slice: x: 2, y: 2, z: 4, core: 2. Of those that a mesh axis runs over, the one named last changes fastest.
Arguments:
- samples: bfloat16 [6144, 2048], P('tm', 'elem'), may hold values from -160 to 160
- taps_weight: bfloat16 [16, 2048, 512], P(None, 'elem'), may hold values from -0.046875 to 0.046875
- retain: float32 [6144], P('tm')
Outputs:
- whitened: float32 [512, 6144], P('elem', 'tm')
All inputs are finite; a program needn't handle non-finite values.
Results may differ from a plain program's by a relative error of at most 0.0003.
Values may be sent and summed in bfloat16 or wider, within the bound.
A program may use at most 192 MiB of HBM per device.

v0:
```python
import jax
import jax.numpy as jnp
from jax import lax
from jax.experimental import pallas as pl
from jax.experimental.pallas import tpu as pltpu
from jax.sharding import PartitionSpec as P

loading_level = 0.1
BLOCK = 128
PIVOTS = 4
LANES = 128


def shifted(array, axis, by):
    size = lax.axis_size(axis)
    pairs = [(i, i + by) for i in range(size) if 0 <= i + by < size]
    return lax.ppermute(array, axis, pairs)


def eliminate(square):
    lane = lax.broadcasted_iota(jnp.int32, (8, LANES), 1)
    groups = [square[8 * g : 8 * g + 8] for g in range(BLOCK // 8)]
    finished = []
    for first in range(0, BLOCK, PIVOTS):
        home = first // 8
        live = range(home, BLOCK // 8)
        inside = (lane >= first) & (lane < first + PIVOTS)
        columns = {
            g: [
                jnp.broadcast_to(groups[g][:, first + j : first + j + 1], (8, LANES))
                for j in range(PIVOTS)
            ]
            for g in live
        }
        offset = first % 8
        pivot = [
            [
                jnp.broadcast_to(columns[home][j][offset + i : offset + i + 1], (8, LANES))
                for j in range(i + 1)
            ]
            for i in range(PIVOTS)
        ]
        rows = [
            jnp.where(
                inside,
                (lane == first + j).astype(jnp.float32),
                jnp.broadcast_to(groups[home][offset + j : offset + j + 1], (8, LANES)),
            )
            for j in range(PIVOTS)
        ]
        inverse, ratio = [], {}
        for j in range(PIVOTS):
            inverse.append(1.0 / pivot[j][j])
            for i in range(j + 1, PIVOTS):
                ratio[i, j] = pivot[i][j] * inverse[j]
            for i in range(j + 1, PIVOTS):
                rows[i] = rows[i] - ratio[i, j] * rows[j]
                for m in range(j + 1, i + 1):
                    pivot[i][m] = pivot[i][m] - ratio[i, j] * pivot[m][j]
        for j in range(PIVOTS):
            finished.append((rows[j] * lax.rsqrt(pivot[j][j]))[:1])
        solved = [rows[j] * inverse[j] for j in range(PIVOTS)]
        for j in reversed(range(PIVOTS)):
            for i in range(j):
                solved[i] = solved[i] - ratio[j, i] * solved[j]
        for g in live:
            change = columns[g][0] * solved[0]
            for j in range(1, PIVOTS):
                change = change + columns[g][j] * solved[j]
            groups[g] = jnp.where(inside, 0.0, groups[g]) - change
    whole = jnp.concatenate(finished, 0)
    row = lax.broadcasted_iota(jnp.int32, (BLOCK, BLOCK), 0)
    column = lax.broadcasted_iota(jnp.int32, (BLOCK, BLOCK), 1)
    return jnp.where(column <= row, whole, 0.0)


def inverse_factor_kernel(covariance_ref, out_ref, work):
    size = covariance_ref.shape[0]
    work[...] = covariance_ref[...]

    @pl.loop(0, size // BLOCK)
    def _(block):
        start = pl.multiple_of(block * BLOCK, BLOCK)
        corner = eliminate(work[pl.ds(start, BLOCK), pl.ds(start, BLOCK)])
        wide_row = lax.broadcasted_iota(jnp.int32, (BLOCK, size), 0)
        wide_column = lax.broadcasted_iota(jnp.int32, (BLOCK, size), 1)
        here = (wide_column >= start) & (wide_column < start + BLOCK)
        strip = jnp.where(
            here, (wide_column == start + wide_row).astype(jnp.float32), work[pl.ds(start, BLOCK), :]
        )
        strip = jnp.dot(
            corner, strip, precision=lax.Precision.HIGHEST, preferred_element_type=jnp.float32
        )
        later = jnp.where(wide_column >= start + BLOCK, strip, 0.0)
        change = lax.dot_general(
            later,
            strip,
            (((0,), (0,)), ((), ())),
            precision=lax.Precision.HIGHEST,
            preferred_element_type=jnp.float32,
        )
        row = lax.broadcasted_iota(jnp.int32, (size, size), 0)
        column = lax.broadcasted_iota(jnp.int32, (size, size), 1)
        cleared = (row >= start + BLOCK) & (column >= start) & (column < start + BLOCK)
        work[...] = jnp.where(cleared, 0.0, work[...]) - change
        out_ref[pl.ds(start, BLOCK), :] = jnp.where(
            wide_column <= start + wide_row, strip, 0.0
        )


def inverse_factor(covariance):
    size = covariance.shape[0]
    return pl.pallas_call(
        inverse_factor_kernel,
        out_shape=jax.ShapeDtypeStruct((size, size), jnp.float32),
        in_specs=[pl.BlockSpec(memory_space=pltpu.VMEM)],
        out_specs=pl.BlockSpec(memory_space=pltpu.VMEM),
        scratch_shapes=[pltpu.VMEM((size, size), jnp.float32)],
        compiler_params=pltpu.CompilerParams(vmem_limit_bytes=32 * 1024 * 1024),
        cost_estimate=pl.CostEstimate(
            flops=12 * size**3, bytes_accessed=8 * size**2, transcendentals=0
        ),
    )(covariance)


def local(samples, taps_weight, retain):
    row_count = samples.shape[0]
    elem_width = samples.shape[1]
    tap_count = taps_weight.shape[0]
    beam_count = taps_weight.shape[2]
    sample_history = shifted(samples[row_count - (tap_count - 1) :], "tm", 1)
    extended = jnp.concatenate([sample_history, samples], 0)
    windowed = jnp.concatenate(
        [
            extended[
                tap_count - 1 - filter_tap_index : tap_count - 1 - filter_tap_index + row_count
            ]
            for filter_tap_index in range(tap_count)
        ],
        1,
    )
    filters = taps_weight.reshape(tap_count * elem_width, beam_count)
    log_retain = jnp.log(retain)
    log_total = jnp.sum(log_retain)
    row_weight = jnp.exp(log_total - jnp.cumsum(log_retain))
    factor = jnp.exp(log_total)
    mass = jnp.sum(row_weight)
    groups = lax.axis_size("elem")
    mine = lax.axis_index("elem")
    blocks = lax.axis_size("tm")
    block = lax.axis_index("tm")
    columns = beam_count // groups
    beam_rows = lax.psum(jnp.dot(windowed, filters, preferred_element_type=jnp.float32), "elem")
    own_columns = lax.dynamic_slice_in_dim(beam_rows, mine * columns, columns, 1)
    gram_rows = lax.dot_general(
        own_columns * row_weight[:, None],
        beam_rows,
        (((0,), (0,)), ((), ())),
        precision=lax.Precision.HIGHEST,
    )
    scalars = jnp.concatenate(
        [jnp.full((4, beam_count), mass), jnp.full((4, beam_count), factor)], 0
    )
    pieces = lax.all_gather(jnp.concatenate([gram_rows, scalars], 0), "tm")
    total = jnp.zeros((columns, beam_count), jnp.float32)
    count = jnp.zeros((1, beam_count), jnp.float32)
    for position in range(blocks):
        decay = pieces[position, columns + 4 : columns + 5]
        taken = position <= block
        total = jnp.where(taken, total * decay + pieces[position, :columns], total)
        count = jnp.where(taken, count * decay + pieces[position, columns : columns + 1], count)
    diagonal = (
        lax.broadcasted_iota(jnp.int32, (columns, beam_count), 1)
        == lax.broadcasted_iota(jnp.int32, (columns, beam_count), 0) + mine * columns
    )
    covariance_rows = total / count + jnp.where(diagonal, loading_level, 0.0)
    covariance = lax.all_gather(covariance_rows, "elem", tiled=True)
    inverse_lower = inverse_factor(covariance)
    local_rows = lax.dynamic_slice_in_dim(inverse_lower, mine * columns, columns, 0)
    return lax.dot_general(
        local_rows, beam_rows, (((1,), (1,)), ((), ())), precision=lax.Precision.HIGHEST
    )


def solution(mesh):
    placed = (P("tm", "elem"), P(None, "elem", None), P("tm"))
    return jax.shard_map(
        local, mesh=mesh, in_specs=placed, out_specs=P("elem", "tm"), check_vma=False
    )
```

profile of v0, /device:TPU:0, one launch (start us, length us, event | category | flops | bytes accessed | tf_op | source)
XLA Modules:
  0.0 202.5 jit_solution(4536108529159138233)
XLA Ops:
  6.5 0.8 slice.127
  7.3 2.3 %collective-permute-start = (bf16[15,512]{1,0:T(8,128)(2,1)S(1)}, bf16[15,512]{1,0:T(8,128)(2,1)S(1)}, u32[]{:S(2)}, u32[]{:S(2)}) collective-permute-start(bf16[15,512]{1,0:T(8,128)(2,1)S(1)} %slice.127), channel_id=1, source_target_pairs={{0,1},{1,2},{2,3},{3,4},{4,5},{5,6},{6,7},{8,9},{9,10},{10,11},{11... | collective-permute-start | bytes 46088 | tf_op jit(solution)/shard_map/ppermute | solution.py:17
  9.7 1.2 constant_dynamic-update-slice_fusion
  10.9 1.3 fusion.3
  12.3 0.2 fusion.5
  12.5 0.2 fusion.7
  12.7 0.2 fusion.9
  12.9 0.2 fusion.11
  13.1 0.2 fusion.13
  13.3 0.2 fusion.15
  13.6 0.2 fusion.19
  13.8 0.2 fusion.21
  14.2 0.2 fusion.25
  14.6 0.2 fusion.1
  15.0 0.3 slice-done
  15.3 1.5 slice-done.1
  16.8 7.8 %fusion.58 = f32[768,512]{1,0:T(8,128)} fusion(bf16[768,8192]{1,0:T(8,128)(2,1)S(1)} %fusion.28, bf16[8192,512]{1,0:T(8,128)(2,1)S(1)} %bitcast.120), kind=kOutput, calls=%fused_computation.91 | convolution fusion | flops 6442450944 | bytes 22544384 | tf_op jit(solution)/shard_map/dot_general | solution.py:153
  24.7 0.6 log_reduce_fusion
  25.3 0.3 reduce-window.9
  26.5 1.3 fusion.53
  27.8 0.5 broadcast_in_dim.21
  28.4 69.6 %all-reduce.2.cloned.1.call-done = f32[768,512]{1,0:T(8,128)} async-done(((f32[768,512]{1,0:T(8,128)}), f32[768,512]{1,0:T(8,128)}) %all-reduce.2.cloned.1.call-update) | async-done | bytes 1572880 | tf_op jit(solution)/shard_map/psum | solution.py:153
  98.0 2.8 %fusion.29 = f32[128,512]{1,0:T(8,128)S(1)} fusion(f32[768,512]{1,0:T(8,128)} %all-reduce.2.cloned.1.call-done, s32[]{:T(128)S(6)} %select_n.156, f32[768]{0:T(1024)S(1)} %get-tuple-element.22), kind=kOutput, calls=%fused_computation.44 | convolution fusion | flops 604078080 | bytes 2231300 | tf_op jit(solution)/shard_map/dot_general | solution.py:155
  100.8 0.8 maximum_maximum_fusion
  101.6 0.2 all-gather.4.cloned.1.call-start
  101.9 27.4 %all-gather.6.cloned.1.call-done = f32[1088,512]{1,0:T(8,128)} async-done(((f32[136,512]{1,0:T(8,128)}), f32[1088,512]{1,0:T(8,128)}) %all-gather.6.cloned.1.call-update) | async-done | bytes 2228240 | tf_op jit(solution)/shard_map/all_gather | solution.py:164
  129.3 1.0 fusion.57
  130.3 2.5 %fusion.35 = f32[128,512]{1,0:T(8,128)} fusion(f32[8,136,512]{2,1,0:T(8,128)} %bitcast.93, s32[128]{0:T(128)S(1)} %iota_add_fusion, f32[512]{0:T(512)S(1)} %add_select_fusion, f32[512]{0:T(512)S(1)} %bitcast.95, f32[512]{0:T(512)S(1)} %bitcast.97, f32[512]{0:T(512)S(1)} %bitcast.99, f32[512]{0:T(512)S(1)} %bitcast.101, f32[512]{0:T(512)S(1)} %bitcast.103, ...), kind=kLoop, calls=%fused_computation.52 | loop fusion | flops 1769472 | bytes 2378248 | tf_op jit(solution)/shard_map/add | solution.py:176
  132.8 28.1 %all-gather.4.cloned.1.call-done.covariance_ref = f32[512,512]{1,0:T(8,128)} async-done(((f32[128,512]{1,0:T(8,128)}), f32[512,512]{1,0:T(8,128)}) %all-gather.4.cloned.1.call-update) | async-done | bytes 1048592 | tf_op jit(solution)/shard_map/all_gather | solution.py:177
  160.9 1.2 copy-done
  162.1 31.4 %shard_map.37 = f32[512,512]{1,0:T(8,128)S(1)} custom-call(f32[512,512]{1,0:T(8,128)S(1)} %copy-done), custom_call_target="tpu_custom_call" | custom-call | flops 1610612736 | bytes 2097152 | tf_op jit(solution)/shard_map/pallas_call | solution.py:113
  193.5 2.5 %fusion.50 = f32[128,768]{1,0:T(8,128)} fusion(f32[768,512]{1,0:T(8,128)S(1)} %copy-done.2, f32[512,512]{1,0:T(8,128)S(1)} %shard_map.37, s32[]{:T(128)S(6)} %select_n.156), kind=kOutput, calls=%fused_computation.74 | convolution fusion | flops 603979776 | bytes 2228228 | tf_op jit(solution)/shard_map/dot_general | solution.py:180
  (28 shorter events, 1.1 us)
Async XLA Ops:
  6.5 5.7 %copy-start.1 = (bf16[768,512]{1,0:T(8,128)(2,1)S(1)}, bf16[768,512]{1,0:T(8,128)(2,1)}, u32[]{:S(2)}) copy-start(bf16[768,512]{1,0:T(8,128)(2,1)} %param.3) | copy-start | bytes 2359300
  6.5 91.5 %all-reduce.2.cloned.1.call-start = ((), (), s32[]{:S(2)}) async-start(), calls=%async_computation | async-start | bytes 3145728 | tf_op jit(solution)/shard_map/psum | solution.py:153
  7.3 3.6 %collective-permute-start = (bf16[15,512]{1,0:T(8,128)(2,1)S(1)}, bf16[15,512]{1,0:T(8,128)(2,1)S(1)}, u32[]{:S(2)}, u32[]{:S(2)}) collective-permute-start(bf16[15,512]{1,0:T(8,128)(2,1)S(1)} %slice.127), channel_id=1, source_target_pairs={{0,1},{1,2},{2,3},{3,4},{4,5},{5,6},{6,7},{8,9},{9,10},{10,11},{11... | collective-permute-start | bytes 46088 | tf_op jit(solution)/shard_map/ppermute | solution.py:17
  13.1 2.2 %slice-start = ((s8[8388608]{0:T(1024)(128)(4,1)}), s8[4194304]{0:T(1024)(128)(4,1)S(1)}, s32[]{:S(2)}) async-start(s8[8388608]{0:T(1024)(128)(4,1)} %bitcast.118), calls=%async_computation.3 | async-start | bytes 8388608
  14.0 2.8 %slice-start.1 = ((s8[8388608]{0:T(1024)(128)(4,1)}), s8[4194304]{0:T(1024)(128)(4,1)S(1)}, s32[]{:S(2)}) async-start(s8[8388608]{0:T(1024)(128)(4,1)} %bitcast.118), calls=%async_computation.4 | async-start | bytes 8388608
  16.8 7.9 %copy-start.3 = (f32[768]{0:T(1024)S(1)}, f32[768]{0:T(1024)}, u32[]{:S(2)}) copy-start(f32[768]{0:T(1024)} %param.5) | copy-start | bytes 9220
  24.6 104.7 %all-gather.6.cloned.1.call-start = ((), (), s32[]{:S(2)}) async-start(), calls=%async_computation.2 | async-start | bytes 2506752 | tf_op jit(solution)/shard_map/all_gather | solution.py:164
  101.6 59.3 %all-gather.4.cloned.1.call-start = ((), (), s32[]{:S(2)}) async-start(), calls=%async_computation.1 | async-start | bytes 1310720 | tf_op jit(solution)/shard_map/all_gather | solution.py:177
  160.9 1.2 copy-start
  162.1 31.4 %copy-start.2 = (f32[768,512]{1,0:T(8,128)S(1)}, f32[768,512]{1,0:T(8,128)}, u32[]{:S(2)}) copy-start(f32[768,512]{1,0:T(8,128)} %all-reduce.2.cloned.1.call-done) | copy-start | bytes 4718596
Sparse Core Ops, SparseCore 0:
  24.7 73.2 all-reduce.1
  101.7 27.5 all-gather.5
  132.9 27.9 all-gather.3
where the time goes:
time: 203 us
  waiting for transfers between devices  125 us (62%)
  Pallas kernels  31.4 us (15%)
  between operations  14.1 us (7%)
  matrix products  13 us (6%)
  other arithmetic  10.4 us (5%)
  local copies, waits for them, and re-layouts  5.87 us (3%)
  starting transfers between devices  2.61 us (1%)
    psum x1, waiting for transfers between devices, local(): lax.psum(jnp.dot(windowed, filters, preferred_element_type=jnp.float32),...  69.6 us
    pallas_call x1, Pallas kernels, inverse_factor(): pl.pallas_call(inverse_factor_kernel, out_shape=jax.ShapeDtypeStruct((siz...  31.4 us
    all_gather x1, waiting for transfers between devices, local(): covariance = lax.all_gather(covariance_rows, 'elem', tiled=True)  28.1 us
    all_gather x1, waiting for transfers between devices, local(): pieces = lax.all_gather(jnp.concatenate([gram_rows, scalars], 0), 'tm')  27.4 us
    dot_general x1, matrix products, local(): jnp.dot(windowed, filters, preferred_element_type=jnp.float32)  7.8 us
    unnamed x13, local copies, waits for them, and re-layouts  4.26 us
  transfers between devices with their start and end apart: 4, of which 3 were waited for; matrix products, arithmetic and copies ran while one was open for 2% of the time, Pallas kernels for 0%

commit v1 on v0

--- a/solution.py
+++ b/solution.py
@@ -151,30 +151,34 @@
     block = lax.axis_index("tm")
     columns = beam_count // groups
     beam_rows = lax.psum(jnp.dot(windowed, filters, preferred_element_type=jnp.float32), "elem")
-    own_columns = lax.dynamic_slice_in_dim(beam_rows, mine * columns, columns, 1)
-    gram_rows = lax.dot_general(
-        own_columns * row_weight[:, None],
-        beam_rows,
-        (((0,), (0,)), ((), ())),
-        precision=lax.Precision.HIGHEST,
-    )
-    scalars = jnp.concatenate(
-        [jnp.full((4, beam_count), mass), jnp.full((4, beam_count), factor)], 0
-    )
-    pieces = lax.all_gather(jnp.concatenate([gram_rows, scalars], 0), "tm")
-    total = jnp.zeros((columns, beam_count), jnp.float32)
-    count = jnp.zeros((1, beam_count), jnp.float32)
+    weighted = beam_rows * row_weight[:, None]
+    strips = [
+        lax.dot_general(
+            weighted[:, start : start + BLOCK],
+            beam_rows[:, start:],
+            (((0,), (0,)), ((), ())),
+            precision=lax.Precision.HIGHEST,
+        )
+        for start in range(0, beam_count, BLOCK)
+    ]
+    packed = jnp.concatenate(strips, 1)
+    width = packed.shape[1]
+    scalars = jnp.concatenate([jnp.full((4, width), mass), jnp.full((4, width), factor)], 0)
+    pieces = lax.all_gather(jnp.concatenate([packed, scalars], 0), "tm")
+    total = jnp.zeros((BLOCK, width), jnp.float32)
+    count = jnp.zeros((1, width), jnp.float32)
     for position in range(blocks):
-        decay = pieces[position, columns + 4 : columns + 5]
+        decay = pieces[position, BLOCK + 4 : BLOCK + 5]
         taken = position <= block
-        total = jnp.where(taken, total * decay + pieces[position, :columns], total)
-        count = jnp.where(taken, count * decay + pieces[position, columns : columns + 1], count)
-    diagonal = (
-        lax.broadcasted_iota(jnp.int32, (columns, beam_count), 1)
-        == lax.broadcasted_iota(jnp.int32, (columns, beam_count), 0) + mine * columns
-    )
-    covariance_rows = total / count + jnp.where(diagonal, loading_level, 0.0)
-    covariance = lax.all_gather(covariance_rows, "elem", tiled=True)
+        total = jnp.where(taken, total * decay + pieces[position, :BLOCK], total)
+        count = jnp.where(taken, count * decay + pieces[position, BLOCK : BLOCK + 1], count)
+    estimate = total / count
+    upper, at = [], 0
+    for start in range(0, beam_count, BLOCK):
+        strip = estimate[:, at : at + beam_count - start]
+        at += beam_count - start
+        upper.append(jnp.pad(strip, ((0, 0), (start, 0))))
+    covariance = jnp.concatenate(upper, 0) + loading_level * jnp.eye(beam_count, dtype=jnp.float32)
     inverse_lower = inverse_factor(covariance)
     local_rows = lax.dynamic_slice_in_dim(inverse_lower, mine * columns, columns, 0)
     return lax.dot_general(

time: 203 us -> 191 us (0.941)
  waiting for transfers between devices: 125 us -> 111 us
    all_gather x2 -> x1, waiting for transfers between devices: 55.5 us -> 41.7 us  [local(): pieces = lax.all_gather(jnp.concatenate([packed, scalars], 0), 'tm')]
    div x0 -> x1, other arithmetic: none -> 3.01 us  [local(): estimate = total / count]
    add x2 -> x1, other arithmetic: 2.5 us -> 0.11 us  [local(): jnp.concatenate(upper, 0)]
    unnamed x13 -> x11, local copies, waits for them, and re-layouts: 4.26 us -> 3.64 us
  transfers between devices with their start and end apart: 4 -> 3, of which waited for: 3 -> 2; matrix products, arithmetic and copies ran while one was open for 2% -> 2% of each run, Pallas kernels for 0% -> 0%
where the time goes in v1:
time: 191 us
  waiting for transfers between devices  111 us (58%)
  Pallas kernels  31.4 us (16%)
  between operations  14.4 us (8%)
  matrix products  14.1 us (7%)
  other arithmetic  12.1 us (6%)
  local copies, waits for them, and re-layouts  5.3 us (3%)
  starting transfers between devices  2.57 us (1%)
    psum x1, waiting for transfers between devices, local(): lax.psum(jnp.dot(windowed, filters, preferred_element_type=jnp.float32),...  69 us
    all_gather x1, waiting for transfers between devices, local(): pieces = lax.all_gather(jnp.concatenate([packed, scalars], 0), 'tm')  41.7 us
    pallas_call x1, Pallas kernels, inverse_factor(): pl.pallas_call(inverse_factor_kernel, out_shape=jax.ShapeDtypeStruct((siz...  31.4 us
    dot_general x1, matrix products, local(): jnp.dot(windowed, filters, preferred_element_type=jnp.float32)  7.78 us
    dot_general x4, matrix products, local(): lax.dot_general(weighted[:, start:start + BLOCK], beam_rows[:, start:], (...  3.84 us
  transfers between devices with their start and end apart: 3, of which 2 were waited for; matrix products, arithmetic and copies ran while one was open for 2% of the time, Pallas kernels for 0%

profile of v1, /device:TPU:0, one launch (start us, length us, event | category | flops | bytes accessed | tf_op | source)
XLA Modules:
  0.0 190.7 jit_solution(15076687861976547021)
XLA Ops:
  6.5 0.8 slice.160
  7.3 2.3 %collective-permute-start = (bf16[15,512]{1,0:T(8,128)(2,1)S(1)}, bf16[15,512]{1,0:T(8,128)(2,1)S(1)}, u32[]{:S(2)}, u32[]{:S(2)}) collective-permute-start(bf16[15,512]{1,0:T(8,128)(2,1)S(1)} %slice.160), channel_id=1, source_target_pairs={{0,1},{1,2},{2,3},{3,4},{4,5},{5,6},{6,7},{8,9},{9,10},{10,11},{11... | collective-permute-start | bytes 46088 | tf_op jit(solution)/shard_map/ppermute | solution.py:17
  9.7 1.2 constant_dynamic-update-slice_fusion
  10.9 0.2 fusion.8
  11.1 0.2 fusion.10
  11.3 0.2 fusion.12
  11.5 0.2 fusion.14
  11.7 0.2 fusion.16
  12.0 0.2 fusion.18
  12.2 0.2 fusion.20
  12.4 0.2 fusion.24
  13.8 0.3 slice-done
  14.1 1.5 slice-done.1
  15.6 7.8 %fusion.66 = f32[768,512]{1,0:T(8,128)} fusion(bf16[768,8192]{1,0:T(8,128)(2,1)S(1)} %fusion.35, bf16[8192,512]{1,0:T(8,128)(2,1)S(1)} %bitcast.78), kind=kOutput, calls=%fused_computation.122 | convolution fusion | flops 6442450944 | bytes 22544384 | tf_op jit(solution)/shard_map/dot_general | solution.py:153
  23.4 0.2 all-gather.3.cloned.1.call-start
  23.7 0.4 copy-done.2
  24.1 0.6 log_reduce_fusion
  24.7 0.3 reduce-window.9
  25.9 1.3 fusion.63
  27.2 0.5 broadcast_in_dim.15
  27.8 69.0 %all-reduce.5.cloned.1.call-done = f32[768,512]{1,0:T(8,128)} async-done(((f32[768,512]{1,0:T(8,128)}), f32[768,512]{1,0:T(8,128)}) %all-reduce.5.cloned.1.call-update) | async-done | bytes 1572880 | tf_op jit(solution)/shard_map/psum | solution.py:153
  96.9 1.7 broadcast_multiply_fusion
  98.8 1.1 fusion.58
  99.9 1.0 fusion
  100.9 0.9 fusion.33
  101.8 0.8 fusion.53
  102.6 1.0 maximum_maximum_fusion
  103.7 41.7 %all-gather.3.cloned.1.call-done = f32[1088,1280]{1,0:T(8,128)} async-done(((f32[136,1280]{1,0:T(8,128)}), f32[1088,1280]{1,0:T(8,128)}) %all-gather.3.cloned.1.call-update) | async-done | bytes 5570576 | tf_op jit(solution)/shard_map/all_gather | solution.py:167
  145.3 1.3 slice_reduce_fusion.7
  146.7 3.0 %fusion.38 = f32[128,1280]{1,0:T(8,128)S(1)} fusion(f32[8,136,1280]{2,1,0:T(8,128)} %bitcast.75, f32[1280]{0:T(1024)S(1)} %add_select_fusion, f32[1280]{0:T(1024)S(1)} %get-tuple-element.6, f32[1280]{0:T(1024)S(1)} %get-tuple-element.8, f32[1280]{0:T(1024)S(1)} %get-tuple-element.10, f32[1280]{0:T(1024)S(1)} %get-tuple-element.12, ...), kind=kLoop, calls=%fused_computation.65 | loop fusion | flops 3932160 | bytes 5944328 | tf_op jit(solution)/shard_map/div | solution.py:175
  149.9 31.4 %shard_map.37 = f32[512,512]{1,0:T(8,128)S(1)} custom-call(f32[512,512]{1,0:T(8,128)S(1)} %fusion.2.covariance_ref), custom_call_target="tpu_custom_call" | custom-call | flops 1610612736 | bytes 2097152 | tf_op jit(solution)/shard_map/pallas_call | solution.py:113
  181.3 2.5 %fusion.60 = f32[128,768]{1,0:T(8,128)} fusion(f32[768,512]{1,0:T(8,128)S(1)} %copy-done.1, f32[512,512]{1,0:T(8,128)S(1)} %shard_map.37, s32[]{:T(128)S(6)} %select_n.175), kind=kOutput, calls=%fused_computation.94 | convolution fusion | flops 603979776 | bytes 2228228 | tf_op jit(solution)/shard_map/dot_general | solution.py:184
  (31 shorter events, 2.0 us)
Async XLA Ops:
  6.5 4.4 %copy-start = (bf16[768,512]{1,0:T(8,128)(2,1)S(1)}, bf16[768,512]{1,0:T(8,128)(2,1)}, u32[]{:S(2)}) copy-start(bf16[768,512]{1,0:T(8,128)(2,1)} %param.3) | copy-start | bytes 2359300
  6.5 90.3 %all-reduce.5.cloned.1.call-start = ((), (), s32[]{:S(2)}) async-start(), calls=%async_computation | async-start | bytes 3145728 | tf_op jit(solution)/shard_map/psum | solution.py:153
  7.3 3.6 %collective-permute-start = (bf16[15,512]{1,0:T(8,128)(2,1)S(1)}, bf16[15,512]{1,0:T(8,128)(2,1)S(1)}, u32[]{:S(2)}, u32[]{:S(2)}) collective-permute-start(bf16[15,512]{1,0:T(8,128)(2,1)S(1)} %slice.160), channel_id=1, source_target_pairs={{0,1},{1,2},{2,3},{3,4},{4,5},{5,6},{6,7},{8,9},{9,10},{10,11},{11... | collective-permute-start | bytes 46088 | tf_op jit(solution)/shard_map/ppermute | solution.py:17
  11.9 2.2 %slice-start = ((s8[8388608]{0:T(1024)(128)(4,1)}), s8[4194304]{0:T(1024)(128)(4,1)S(1)}, s32[]{:S(2)}) async-start(s8[8388608]{0:T(1024)(128)(4,1)} %bitcast.76), calls=%async_computation.2 | async-start | bytes 8388608
  12.8 2.8 %slice-start.1 = ((s8[8388608]{0:T(1024)(128)(4,1)}), s8[4194304]{0:T(1024)(128)(4,1)S(1)}, s32[]{:S(2)}) async-start(s8[8388608]{0:T(1024)(128)(4,1)} %bitcast.76), calls=%async_computation.3 | async-start | bytes 8388608
  23.4 0.7 copy-start.2
  23.4 121.9 %all-gather.3.cloned.1.call-start = ((), (), s32[]{:S(2)}) async-start(), calls=%async_computation.1 | async-start | bytes 6266880 | tf_op jit(solution)/shard_map/all_gather | solution.py:167
  96.9 1.9 copy-start.1
Sparse Core Ops, SparseCore 0:
  23.6 73.2 all-reduce.4
  103.8 41.5 all-gather.2

commit v2 on v1

--- a/solution.py
+++ b/solution.py
@@ -1,3 +1,5 @@
+import functools
+
 import jax
 import jax.numpy as jnp
 from jax import lax
@@ -9,6 +11,9 @@
 BLOCK = 128
 PIVOTS = 4
 LANES = 128
+CHUNK = 64
+LAG = 3
+MESH = pl.DeviceIdType.MESH
 
 
 def shifted(array, axis, by):
@@ -123,6 +128,145 @@
     )(covariance)
 
 
+def line_sum_kernel(size, partial_ref, out_ref, arriving, running, in_sem, up_sem, down_sem, fan_sem):
+    me = lax.axis_index("elem")
+    root = size // 2
+    side = jnp.where(me < root, 0, 1)
+    toward = jnp.where(me < root, me + 1, me - 1)
+    outward = jnp.where(me < root, me - 1, me + 1)
+    at_root = me == root
+    at_end = (me == 0) | (me == size - 1)
+    inner = jnp.logical_not(at_root | at_end)
+    chunks = partial_ref.shape[0] // CHUNK
+
+    barrier = pltpu.get_barrier_semaphore()
+
+    @pl.when(me > 0)
+    def _():
+        pl.semaphore_signal(barrier, inc=1, device_id={"elem": me - 1}, device_id_type=MESH)
+
+    @pl.when(me < size - 1)
+    def _():
+        pl.semaphore_signal(barrier, inc=1, device_id={"elem": me + 1}, device_id_type=MESH)
+
+    @pl.when(at_end)
+    def _():
+        pl.semaphore_wait(barrier, 1)
+
+    @pl.when(jnp.logical_not(at_end))
+    def _():
+        pl.semaphore_wait(barrier, 2)
+
+    def rows(chunk):
+        return pl.ds(pl.multiple_of(chunk * CHUNK, CHUNK), CHUNK)
+
+    def inward(source, chunk):
+        return pltpu.make_async_remote_copy(
+            src_ref=source.at[rows(chunk)],
+            dst_ref=arriving.at[side, rows(chunk)],
+            send_sem=up_sem.at[chunk],
+            recv_sem=in_sem.at[side, chunk],
+            device_id={"elem": toward},
+            device_id_type=MESH,
+        )
+
+    def arrival(which, chunk):
+        return pltpu.make_async_remote_copy(
+            src_ref=partial_ref.at[rows(chunk)],
+            dst_ref=arriving.at[which, rows(chunk)],
+            send_sem=up_sem.at[chunk],
+            recv_sem=in_sem.at[which, chunk],
+            device_id={"elem": toward},
+            device_id_type=MESH,
+        )
+
+    def back(target, way, chunk):
+        return pltpu.make_async_remote_copy(
+            src_ref=out_ref.at[rows(chunk)],
+            dst_ref=out_ref.at[rows(chunk)],
+            send_sem=fan_sem.at[way, chunk],
+            recv_sem=down_sem.at[chunk],
+            device_id={"elem": target},
+            device_id_type=MESH,
+        )
+
+    @pl.when(at_end)
+    def _():
+        @pl.loop(0, chunks)
+        def _(chunk):
+            inward(partial_ref, chunk).start()
+
+        @pl.loop(0, chunks)
+        def _(chunk):
+            back(toward, 0, chunk).wait_recv()
+            inward(partial_ref, chunk).wait_send()
+
+    @pl.when(inner)
+    def _():
+        def pass_on(chunk):
+            back(toward, 0, chunk).wait_recv()
+            back(outward, 0, chunk).start()
+
+        @pl.loop(0, chunks)
+        def _(chunk):
+            arrival(side, chunk).wait_recv()
+            running[rows(chunk), :] = partial_ref[rows(chunk), :] + arriving[side, rows(chunk), :]
+            inward(running, chunk).start()
+
+            @pl.when(chunk >= LAG)
+            def _():
+                pass_on(chunk - LAG)
+
+        @pl.loop(chunks - LAG, chunks)
+        def _(chunk):
+            pass_on(chunk)
+
+        @pl.loop(0, chunks)
+        def _(chunk):
+            inward(running, chunk).wait_send()
+            back(outward, 0, chunk).wait_send()
+
+    @pl.when(at_root)
+    def _():
+        @pl.loop(0, chunks)
+        def _(chunk):
+            arrival(0, chunk).wait_recv()
+            arrival(1, chunk).wait_recv()
+            out_ref[rows(chunk), :] = partial_ref[rows(chunk), :] + (
+                arriving[0, rows(chunk), :] + arriving[1, rows(chunk), :]
+            )
+            back(root - 1, 0, chunk).start()
+            back(root + 1, 1, chunk).start()
+
+        @pl.loop(0, chunks)
+        def _(chunk):
+            back(root - 1, 0, chunk).wait_send()
+            back(root + 1, 1, chunk).wait_send()
+
+
+def line_sum(partial):
+    size = lax.axis_size("elem")
+    row_count, width = partial.shape
+    chunks = row_count // CHUNK
+    return pl.pallas_call(
+        functools.partial(line_sum_kernel, size),
+        out_shape=jax.ShapeDtypeStruct(partial.shape, jnp.float32),
+        in_specs=[pl.BlockSpec(memory_space=pltpu.VMEM)],
+        out_specs=pl.BlockSpec(memory_space=pltpu.VMEM),
+        scratch_shapes=[
+            pltpu.VMEM((2, row_count, width), jnp.float32),
+            pltpu.VMEM((row_count, width), jnp.float32),
+            pltpu.SemaphoreType.DMA((2, chunks)),
+            pltpu.SemaphoreType.DMA((chunks,)),
+            pltpu.SemaphoreType.DMA((chunks,)),
+            pltpu.SemaphoreType.DMA((2, chunks)),
+        ],
+        compiler_params=pltpu.CompilerParams(
+            collective_id=0, has_side_effects=True, vmem_limit_bytes=32 * 1024 * 1024
+        ),
+    )(partial)
+
+
 def local(samples, taps_weight, retain):
     row_count = samples.shape[0]
     elem_width = samples.shape[1]
@@ -150,7 +294,7 @@
     blocks = lax.axis_size("tm")
     block = lax.axis_index("tm")
     columns = beam_count // groups
-    beam_rows = lax.psum(jnp.dot(windowed, filters, preferred_element_type=jnp.float32), "elem")
+    beam_rows = line_sum(jnp.dot(windowed, filters, preferred_element_type=jnp.float32))
     weighted = beam_rows * row_weight[:, None]
     strips = [
         lax.dot_general(

time: 191 us -> 187 us (0.979)
  waiting for transfers between devices: 111 us -> 40.4 us
  Pallas kernels: 31.4 us -> 84.7 us
  other arithmetic: 12.1 us -> 24.7 us
    psum x1 -> x0, waiting for transfers between devices: 69 us -> none  [local(): lax.psum(jnp.dot(windowed, filters, preferred_element_type=jnp.float32),...]
    pallas_call x0 -> x1, Pallas kernels: none -> 53.3 us  [line_sum(): pl.pallas_call(functools.partial(line_sum_kernel, size), out_shape=jax.Sh...]
    unnamed x15, other arithmetic: 2.57 us -> 15.6 us
  transfers between devices with their start and end apart: 3 -> 2, of which waited for: 2 -> 1; matrix products, arithmetic and copies ran while one was open for 2% -> 3% of each run, Pallas kernels for 0% -> 0%
where the time goes in v2:
time: 187 us; the launch traced here: 186 us
  Pallas kernels  84.7 us (45%)
  waiting for transfers between devices  40.4 us (22%)
  other arithmetic  24.7 us (13%)
  matrix products  15.8 us (8%)
  between operations  14.3 us (8%)
  local copies, waits for them, and re-layouts  3.9 us (2%)
  starting transfers between devices  2.35 us (1%)
    pallas_call x1, Pallas kernels, line_sum(): pl.pallas_call(functools.partial(line_sum_kernel, size), out_shape=jax.Sh...  53.3 us
    all_gather x1, waiting for transfers between devices, local(): pieces = lax.all_gather(jnp.concatenate([packed, scalars], 0), 'tm')  40.4 us
    pallas_call x1, Pallas kernels, inverse_factor(): pl.pallas_call(inverse_factor_kernel, out_shape=jax.ShapeDtypeStruct((siz...  31.4 us
    unnamed x15, other arithmetic  15.6 us
    dot_general x1, matrix products, local(): jnp.dot(windowed, filters, preferred_element_type=jnp.float32)  9.52 us
    dot_general x4, matrix products, local(): lax.dot_general(weighted[:, start:start + BLOCK], beam_rows[:, start:], (...  3.85 us
  transfers between devices with their start and end apart: 2, of which 1 were waited for; matrix products, arithmetic and copies ran while one was open for 3% of the time, Pallas kernels for 0%

profile of v2, /device:TPU:0, one launch (start us, length us, event | category | flops | bytes accessed | tf_op | source)
XLA Modules:
  0.0 186.2 jit_solution(850958014079098995)
XLA Ops:
  6.5 0.8 slice.160
  7.3 2.3 %collective-permute-start = (bf16[15,512]{1,0:T(8,128)(2,1)S(1)}, bf16[15,512]{1,0:T(8,128)(2,1)S(1)}, u32[]{:S(2)}, u32[]{:S(2)}) collective-permute-start(bf16[15,512]{1,0:T(8,128)(2,1)S(1)} %slice.160), channel_id=1, source_target_pairs={{0,1},{1,2},{2,3},{3,4},{4,5},{5,6},{6,7},{8,9},{9,10},{10,11},{11... | collective-permute-start | bytes 46088 | tf_op jit(solution)/shard_map/ppermute | solution.py:22
  9.7 2.1 %constant_dynamic-update-slice_fusion = bf16[768,8192]{1,0:T(8,128)(2,1)} fusion(bf16[768,512]{1,0:T(8,128)(2,1)} %param.3), kind=kLoop, calls=%fused_computation.96 | loop fusion | bytes 1572864
  11.8 0.6 log_reduce_fusion
  12.9 1.3 fusion.63
  15.7 1.1 fusion.8
  16.9 1.1 fusion.10
  18.0 1.1 fusion.12
  19.1 1.2 fusion.14
  20.3 1.1 fusion.16
  21.4 1.2 fusion.18
  22.6 1.1 fusion.20
  23.7 1.0 fusion.22
  24.7 1.1 fusion.24
  25.8 1.1 fusion.26
  26.9 1.1 fusion.28
  28.0 1.1 fusion.30
  29.1 1.1 fusion.32
  30.2 1.1 fusion.6
  31.4 1.2 fusion.33
  32.5 9.5 %fusion.66.partial_ref = f32[768,512]{1,0:T(8,128)S(1)} fusion(bf16[768,8192]{1,0:T(8,128)(2,1)} %fusion.33, bf16[8192,512]{1,0:T(8,128)(2,1)S(1)} %bitcast.78), kind=kOutput, calls=%fused_computation.122 | convolution fusion | flops 6442450944 | bytes 22544384 | tf_op jit(solution)/shard_map/dot_general | solution.py:297
  42.1 53.3 %shard_map.37 = f32[768,512]{1,0:T(8,128)S(1)} custom-call(f32[768,512]{1,0:T(8,128)S(1)} %fusion.66.partial_ref), custom_call_target="tpu_custom_call" | custom-call | tf_op jit(solution)/shard_map/pallas_call | solution.py:251
  95.6 1.1 fusion.57
  96.7 1.0 fusion
  97.7 0.9 fusion.34
  98.6 0.8 fusion.53
  99.4 1.0 maximum_maximum_fusion
  100.5 40.4 %all-gather.3.cloned.1.call-done = f32[1088,1280]{1,0:T(8,128)} async-done(((f32[136,1280]{1,0:T(8,128)}), f32[1088,1280]{1,0:T(8,128)}) %all-gather.3.cloned.1.call-update) | async-done | bytes 5570576 | tf_op jit(solution)/shard_map/all_gather | solution.py:311
  140.9 1.3 slice_reduce_fusion.7
  142.3 3.0 %fusion.38 = f32[128,1280]{1,0:T(8,128)S(1)} fusion(f32[8,136,1280]{2,1,0:T(8,128)} %bitcast.75, f32[1280]{0:T(1024)S(1)} %add_select_fusion, f32[1280]{0:T(1024)S(1)} %get-tuple-element.6, f32[1280]{0:T(1024)S(1)} %get-tuple-element.8, f32[1280]{0:T(1024)S(1)} %get-tuple-element.10, f32[1280]{0:T(1024)S(1)} %get-tuple-element.12, ...), kind=kLoop, calls=%fused_computation.65 | loop fusion | flops 3932160 | bytes 5944328 | tf_op jit(solution)/shard_map/div | solution.py:319
  145.5 31.4 %shard_map.38 = f32[512,512]{1,0:T(8,128)S(1)} custom-call(f32[512,512]{1,0:T(8,128)S(1)} %fusion.2.covariance_ref), custom_call_target="tpu_custom_call" | custom-call | flops 1610612736 | bytes 2097152 | tf_op jit(solution)/shard_map/pallas_call | solution.py:118
  176.9 2.5 %fusion.60 = f32[128,768]{1,0:T(8,128)} fusion(f32[768,512]{1,0:T(8,128)S(1)} %shard_map.37, f32[512,512]{1,0:T(8,128)S(1)} %shard_map.38, s32[]{:T(128)S(6)} %select_n.175), kind=kOutput, calls=%fused_computation.94 | convolution fusion | flops 603979776 | bytes 2228228 | tf_op jit(solution)/shard_map/dot_general | solution.py:328
  (27 shorter events, 1.6 us)
Async XLA Ops:
  6.5 9.2 %copy-start = (bf16[768,512]{1,0:T(8,128)(2,1)S(1)}, bf16[768,512]{1,0:T(8,128)(2,1)}, u32[]{:S(2)}) copy-start(bf16[768,512]{1,0:T(8,128)(2,1)} %param.3) | copy-start | bytes 2359300
  6.5 5.3 %copy-start.1 = (f32[768]{0:T(1024)S(1)}, f32[768]{0:T(1024)}, u32[]{:S(2)}) copy-start(f32[768]{0:T(1024)} %param.5) | copy-start | bytes 9220
  6.5 134.4 %all-gather.3.cloned.1.call-start = ((), (), s32[]{:S(2)}) async-start(), calls=%async_computation | async-start | bytes 6266880 | tf_op jit(solution)/shard_map/all_gather | solution.py:311
  7.3 8.4 %collective-permute-start = (bf16[15,512]{1,0:T(8,128)(2,1)S(1)}, bf16[15,512]{1,0:T(8,128)(2,1)S(1)}, u32[]{:S(2)}, u32[]{:S(2)}) collective-permute-start(bf16[15,512]{1,0:T(8,128)(2,1)S(1)} %slice.160), channel_id=1, source_target_pairs={{0,1},{1,2},{2,3},{3,4},{4,5},{5,6},{6,7},{8,9},{9,10},{10,11},{11... | collective-permute-start | bytes 46088 | tf_op jit(solution)/shard_map/ppermute | solution.py:22
  21.4 11.1 %slice-start = ((s8[8388608]{0:T(1024)(128)(4,1)}), s8[4194304]{0:T(1024)(128)(4,1)S(1)}, s32[]{:S(2)}) async-start(s8[8388608]{0:T(1024)(128)(4,1)} %bitcast.76), calls=%async_computation.1 | async-start | bytes 8388608
  26.9 5.6 %slice-start.1 = ((s8[8388608]{0:T(1024)(128)(4,1)}), s8[4194304]{0:T(1024)(128)(4,1)S(1)}, s32[]{:S(2)}) async-start(s8[8388608]{0:T(1024)(128)(4,1)} %bitcast.76), calls=%async_computation.2 | async-start | bytes 8388608
Sparse Core Ops, SparseCore 0:
  100.6 40.2 all-gather.2
